TPU v7x, 32 devices: a whole 2x2x4 slice. The times are simulated.
32 devices in a mesh: tile: 8 (over z, y), grp: 4 (over x, core).
Axes of the slice: x: 2, y: 2, z: 4, core: 2. Of those that a mesh axis runs over, the one named last changes fastest.
Arguments:
- soil_water: float32 [6, 2097152], P(None, ('tile', 'grp')), may hold values from 0.1 to 0.9
- rainfall: float32 [2097152], P(('tile', 'grp')), may hold values from 0.005 to 0.2
- drain_coef: float32 [6, 2097152], P(None, ('tile', 'grp')), may hold values from 0.02 to 0.5
- cell_storage: float32 [2097152], P(('tile', 'grp')), may hold values from 0.01 to 2
- release_rate: float32 [2097152], P(('tile', 'grp')), may hold values from 0.05 to 0.8
- downstream: int32 [2097152], P(('tile', 'grp')), may hold values from 1 to 128, as said below
- block_owner: int32 [16384, 1], P(('tile', 'grp')), may hold values from 0 to 31; in each aligned block of 512 rows (0 to 511, 512 to 1023, ...) at most 32 rows name the same one
- outlet_reach: int32 [16384], P(('tile', 'grp')), may hold values from 0 to 127
- river_storage: float32 [4, 1024], P('grp', 'tile'), may hold values from 0.02 to 0.5
- river_lag: float32 [4, 1024], P('grp', 'tile'), may hold values from 0 to 1
Outputs:
- soil_out: float32 [6, 2097152], P(None, ('tile', 'grp'))
- storage_out: float32 [2097152], P(('tile', 'grp'))
- section: float32 [4, 1024], P('grp', 'tile')
Inputs may be any that keep to these rules, and one draw needn't show every extreme that they name: `downstream`: within its block of 128 cells a cell drains to a later cell of the block, or to 128, the block's outlet. `block_owner`: of the 512 blocks of one device, at most 32 have the same owner.
All inputs are finite; a program needn't handle non-finite values.
Results may differ from a plain program's by a relative error of at most 0.0003.
Values sent between devices are 32-bit elements; how exact they have to be, the bound alone decides.
A program may use at most 64 MiB of HBM per device.

v0:
```python
import functools
import math

import jax
import jax.numpy as jnp
from jax import lax
from jax.experimental import pallas as pl
from jax.experimental.pallas import tpu as pltpu
from jax.sharding import PartitionSpec as P

SUB = 4
MOMENTS = SUB * (SUB + 1) // 2
MESH = pl.DeviceIdType.MESH

recharge_share = 0.2


def split(x):
    high = x.astype(jnp.bfloat16)
    low = (x - high.astype(jnp.float32)).astype(jnp.bfloat16)
    return high, low


def lanes_of(shape):
    return lax.broadcasted_iota(jnp.int32, shape, len(shape) - 1)


def pick(values, index):
    return jnp.take_along_axis(values, index, axis=1)


def sort_rows(key, lane):
    width = key.shape[1]
    size = 2
    while size <= width:
        step = size // 2
        while step:
            other = pick(key, lane ^ step)
            low = ((lane & step) != 0) == ((lane & size) != 0)
            key = jnp.where(low, jnp.minimum(key, other), jnp.maximum(key, other))
            step //= 2
        size *= 2
    return key


def route_kernel(
    share_ref, storage_ref, rate_ref, down_ref, owner_ref, reach_ref, up_ref, agg_ref, moment_ref
):
    step = pl.program_id(0)
    rows, width = share_ref.shape
    devices, _, reaches = agg_ref.shape
    blocks = owner_ref.shape[1]
    lane = lanes_of((rows, width))
    down = down_ref[...]
    key = sort_rows((down * width + lane).astype(jnp.float32), lane).astype(jnp.int32)
    order = key % width
    target = key // width
    ends = jnp.zeros_like(lane)
    hop = width // 2
    while hop:
        ends = jnp.where(pick(target, ends + (hop - 1)) <= lane, ends + hop, ends)
        hop //= 2
    square = (width, width)
    before = (lax.broadcasted_iota(jnp.int32, square, 0) < lanes_of(square)).astype(jnp.bfloat16)
    share = share_ref[...]
    rate = rate_ref[...]
    storage = storage_ref[...]
    leaving = jnp.where(down == width, rate, 0.0)
    powers = [leaving]
    for _ in range(SUB - 1):
        powers.append(powers[-1] * leaving)
    sums = jnp.zeros((rows, width), jnp.float32)
    column = 0
    for power in powers:
        value = jnp.sum(power * storage, axis=1, keepdims=True)
        sums = jnp.where(lane == column, value, sums)
        column += 1
    for turn in range(SUB):
        release = rate * storage
        high, low = split(pick(release, order))
        running = jnp.dot(high, before, preferred_element_type=jnp.float32) + jnp.dot(
            low, before, preferred_element_type=jnp.float32
        )
        upto = pick(running, ends)
        upstream = jnp.where(lane == 0, 0.0, upto - pltpu.roll(upto, 1, 1))
        gained = share + upstream
        up_ref[turn] = gained
        storage = storage + gained - release
        for power in powers[: SUB - 1 - turn]:
            value = jnp.sum(power * gained, axis=1, keepdims=True)
            sums = jnp.where(lane == column, value, sums)
            column += 1
    moment_ref[pl.ds(pl.multiple_of(step * rows, rows), rows), :] = sums

    @pl.when(step == pl.num_programs(0) - 1)
    def _():
        flat = moment_ref[...].T[:16]
        mine = lax.broadcasted_iota(jnp.int32, (devices, blocks), 0) == owner_ref[...]
        mine = mine.astype(jnp.float32)[:, None, :]
        hits = lax.broadcasted_iota(jnp.int32, (reaches, blocks), 0) == reach_ref[...]
        hits = hits.astype(jnp.float32).astype(jnp.bfloat16)
        total = jnp.zeros((devices * 16, reaches), jnp.float32)
        for part in split(flat):
            spread = (mine * part.astype(jnp.float32)[None]).reshape(devices * 16, blocks)
            total = total + lax.dot_general(
                spread.astype(jnp.bfloat16),
                hits,
                (((1,), (1,)), ((), ())),
                preferred_element_type=jnp.float32,
            )
        agg_ref[...] = total.reshape(devices, 16, reaches)[:, :MOMENTS, :]


def exchange_kernel(
    groups,
    devices,
    agg_ref,
    volume_ref,
    lag_ref,
    out_ref,
    landed,
    mine,
    send_sem,
    recv_sem,
    send_all,
    recv_all,
):
    me = lax.axis_index("tile") * groups + lax.axis_index("grp")

    def peer_at(step):
        peer = lax.rem(me + step, devices)
        return peer, (peer // groups, lax.rem(peer, groups))

    barrier = pltpu.get_barrier_semaphore()

    def greet(step, carry):
        pl.semaphore_signal(barrier, inc=1, device_id=peer_at(step)[1], device_id_type=MESH)
        return carry

    lax.fori_loop(1, devices, greet, 0)
    pl.semaphore_wait(barrier, devices - 1)

    def part(step):
        peer, place = peer_at(step)
        return pltpu.make_async_remote_copy(
            src_ref=agg_ref.at[peer],
            dst_ref=landed.at[step],
            send_sem=send_sem.at[step],
            recv_sem=recv_sem.at[step],
            device_id=place,
            device_id_type=MESH,
        )

    def whole(step):
        return pltpu.make_async_remote_copy(
            src_ref=mine,
            dst_ref=out_ref.at[me],
            send_sem=send_all.at[step],
            recv_sem=recv_all.at[step],
            device_id=peer_at(step)[1],
            device_id_type=MESH,
        )

    def start(copy):
        def body(step, carry):
            copy(step).start()
            return carry

        lax.fori_loop(1, devices, body, 0)

    def finish(copy):
        def body(step, carry):
            copy(step).wait()
            return carry

        lax.fori_loop(1, devices, body, 0)

    start(part)
    landed[0] = agg_ref[me]
    finish(part)
    mine[pl.ds(0, MOMENTS), :] = jnp.sum(landed[...], axis=0)
    mine[pl.ds(MOMENTS, 1), :] = volume_ref[...]
    mine[pl.ds(MOMENTS + 1, 1), :] = lag_ref[...]
    start(whole)
    out_ref[me] = mine[...]
    finish(whole)


def simulate(groups, river, width):
    devices, reaches = river[0].shape
    shape = (devices, reaches)
    lane = lanes_of(shape)
    row = lax.broadcasted_iota(jnp.int32, shape, 0)
    volume, lag = river[MOMENTS], river[MOMENTS + 1]
    weight = 1.0 / (1.0 + lag)
    held = list(river[:SUB])
    gained, at = [], SUB
    for turn in range(SUB - 1):
        gained.append(river[at : at + SUB - 1 - turn])
        at += SUB - 1 - turn

    def ladder(gain, place, axis, first, size):
        steps, step = [], first
        while step < size:
            inside = place >= step
            steps.append((step, jnp.where(inside, gain, 0.0)))
            gain = jnp.where(inside, gain * pltpu.roll(gain, step, axis), gain)
            step *= 2
        return steps, gain

    def climb(steps, value, axis):
        for step, gain in steps:
            value = value + gain * pltpu.roll(value, step, axis)
        return value

    def last(value):
        return jnp.broadcast_to(value[:, reaches - 1 :], shape)

    within, gain = ladder(weight, lane, 1, 1, reaches)
    across, _ = ladder(last(gain), row, 0, groups, devices)
    backs, flow = [], volume
    for turn in range(SUB):
        back = 1.0 / (1.0 + volume)
        backs.append(back)
        feed = weight * (volume + back * held[0] / width)
        offset = climb(within, feed, 1)
        head = climb(across, last(offset), 0)
        if devices > groups:
            head = jnp.where(row >= groups, pltpu.roll(head, groups, 0), 0.0)
        else:
            head = jnp.zeros_like(head)
        flow = gain * head + offset
        volume = lag * flow
        if turn < SUB - 1:
            held = [
                held[j] + gained[turn][j] - back * held[j + 1] for j in range(SUB - 1 - turn)
            ]
    return backs, flow


def settle_kernel(
    groups,
    river_ref,
    storage_ref,
    rate_ref,
    down_ref,
    owner_ref,
    reach_ref,
    up_ref,
    storage_out_ref,
    section_ref,
    table_ref,
    place_ref,
):
    step = pl.program_id(0)
    rows, width = storage_ref.shape
    devices, _, reaches = river_ref.shape
    blocks = owner_ref.shape[1]

    @pl.when(step == 0)
    def _():
        river = [river_ref[:, m, :] for m in range(MOMENTS + 2)]
        backs, flow = simulate(groups, river, width)
        me = lax.axis_index("tile") * groups + lax.axis_index("grp")
        own = lax.broadcasted_iota(jnp.int32, flow.shape, 0) == me
        section_ref[...] = jnp.log1p(jnp.sum(jnp.where(own, flow, 0.0), axis=0, keepdims=True))
        for turn in range(SUB):
            high, low = split(backs[turn])
            table_ref[0, :, turn * reaches : (turn + 1) * reaches] = high
            table_ref[1, :, turn * reaches : (turn + 1) * reaches] = low
        both = jnp.concatenate(
            [
                jnp.broadcast_to(owner_ref[...].astype(jnp.float32), (8, blocks)),
                jnp.broadcast_to(reach_ref[...].astype(jnp.float32), (8, blocks)),
                jnp.zeros((112, blocks), jnp.float32),
            ],
            axis=0,
        )
        place_ref[...] = both.T

    place = place_ref[pl.ds(pl.multiple_of(step * rows, rows), rows), :].astype(jnp.int32)
    owner, reach = place[:, 0:1], place[:, 8:9]
    mine = (lanes_of((rows, devices)) == owner).astype(jnp.float32).astype(jnp.bfloat16)
    found = jnp.dot(mine, table_ref[0], preferred_element_type=jnp.float32) + jnp.dot(
        mine, table_ref[1], preferred_element_type=jnp.float32
    )
    hit = lanes_of((rows, reaches)) == reach
    leaving = down_ref[...] == width
    rate = rate_ref[...]
    storage = storage_ref[...]
    for turn in range(SUB):
        back = jnp.sum(
            jnp.where(hit, found[:, turn * reaches : (turn + 1) * reaches], 0.0),
            axis=1,
            keepdims=True,
        )
        release = rate * storage * jnp.where(leaving, back, 1.0)
        storage = storage + up_ref[turn] - release
    storage_out_ref[...] = storage


def land_step(soil_water, rainfall, drain_coef):
    top_layer = soil_water[0]
    surface = rainfall * top_layer * top_layer
    soaked = rainfall - surface
    drained = drain_coef * soil_water * soil_water * soil_water
    inflow = jnp.concatenate([soaked[None], drained[:-1]], axis=0)
    return (soil_water + inflow - drained, surface + drained[-1])


def local(
    soil_water,
    rainfall,
    drain_coef,
    cell_storage,
    release_rate,
    downstream,
    block_owner,
    outlet_reach,
    river_storage,
    river_lag,
):
    groups = lax.axis_size("grp")
    devices = lax.axis_size("tile") * groups
    blocks = block_owner.shape[0]
    width = rainfall.shape[0] // blocks
    reaches = river_storage.shape[1]
    rows = math.gcd(blocks, 64)
    soil_mid, runoff = land_step(soil_water, rainfall, drain_coef)
    share = (runoff / SUB).reshape(blocks, width)
    storage = cell_storage.reshape(blocks, width)
    rate = release_rate.reshape(blocks, width)
    down = downstream.reshape(blocks, width)
    owner = block_owner.reshape(1, blocks)
    reach = outlet_reach.reshape(1, blocks)

    tile = pl.BlockSpec((rows, width), lambda i: (i, 0))
    line = pl.BlockSpec((1, blocks), lambda i: (0, 0))
    stack = pl.BlockSpec((SUB, rows, width), lambda i: (0, i, 0))
    gained, agg = pl.pallas_call(
        route_kernel,
        grid=(blocks // rows,),
        out_shape=(
            jax.ShapeDtypeStruct((SUB, blocks, width), jnp.float32),
            jax.ShapeDtypeStruct((devices, MOMENTS, reaches), jnp.float32),
        ),
        in_specs=[tile, tile, tile, tile, line, line],
        out_specs=(stack, pl.BlockSpec((devices, MOMENTS, reaches), lambda i: (0, 0, 0))),
        scratch_shapes=[pltpu.VMEM((blocks, width), jnp.float32)],
        compiler_params=pltpu.CompilerParams(vmem_limit_bytes=40 * 1024 * 1024),
    )(share, storage, rate, down, owner, reach)

    vmem = pl.BlockSpec(memory_space=pltpu.VMEM)
    river = pl.pallas_call(
        functools.partial(exchange_kernel, groups, devices),
        out_shape=jax.ShapeDtypeStruct((devices, MOMENTS + 2, reaches), jnp.float32),
        in_specs=[vmem] * 3,
        out_specs=vmem,
        scratch_shapes=[
            pltpu.VMEM((devices, MOMENTS, reaches), jnp.float32),
            pltpu.VMEM((MOMENTS + 2, reaches), jnp.float32),
            pltpu.SemaphoreType.DMA((devices,)),
            pltpu.SemaphoreType.DMA((devices,)),
            pltpu.SemaphoreType.DMA((devices,)),
            pltpu.SemaphoreType.DMA((devices,)),
        ],
        compiler_params=pltpu.CompilerParams(
            collective_id=0, has_side_effects=True, vmem_limit_bytes=40 * 1024 * 1024
        ),
    )(agg, river_storage, river_lag)

    storage_out, section = pl.pallas_call(
        functools.partial(settle_kernel, groups),
        grid=(blocks // rows,),
        out_shape=(
            jax.ShapeDtypeStruct((blocks, width), jnp.float32),
            jax.ShapeDtypeStruct((1, reaches), jnp.float32),
        ),
        in_specs=[
            pl.BlockSpec((devices, MOMENTS + 2, reaches), lambda i: (0, 0, 0)),
            tile,
            tile,
            tile,
            line,
            line,
            stack,
        ],
        out_specs=(tile, pl.BlockSpec((1, reaches), lambda i: (0, 0))),
        scratch_shapes=[
            pltpu.VMEM((2, devices, SUB * reaches), jnp.bfloat16),
            pltpu.VMEM((blocks, 128), jnp.float32),
        ],
        compiler_params=pltpu.CompilerParams(vmem_limit_bytes=40 * 1024 * 1024),
    )(river, storage, rate, down, owner, reach, gained)

    storage_out = storage_out.reshape(-1)
    flooded = storage_out / (storage_out + 1.0)
    soil_out = soil_mid.at[0].add(recharge_share * flooded * (1.0 - soil_mid[0]))
    return (soil_out, storage_out, section)


def solution(mesh):
    placed = (
        P(None, ("tile", "grp")),
        P(("tile", "grp")),
        P(None, ("tile", "grp")),
        P(("tile", "grp")),
        P(("tile", "grp")),
        P(("tile", "grp")),
        P(("tile", "grp"), None),
        P(("tile", "grp")),
        P("grp", "tile"),
        P("grp", "tile"),
    )
    return jax.shard_map(
        local,
        mesh=mesh,
        in_specs=placed,
        out_specs=(P(None, ("tile", "grp")), P(("tile", "grp")), P("grp", "tile")),
        check_vma=False,
    )
```

profile of v0, /device:TPU:0, one launch (start us, length us, event | category | flops | bytes accessed | tf_op | source)
XLA Modules:
  0.0 65.7 jit_solution(12871666433660594555)
XLA Ops:
  0.6 0.0 slice-start
  0.6 0.0 copy-start.9
  0.7 0.0 copy-start.7
  0.7 2.6 %multiply_multiply_fusion = f32[6,65536]{1,0:T(8,128)S(1)} fusion(f32[6,65536]{1,0:T(8,128)} %param.12, f32[6,65536]{1,0:T(8,128)} %param.14), kind=kLoop, calls=%fused_computation | loop fusion | flops 1179648 | bytes 4718592 | tf_op jit(solution)/shard_map/mul | solution.py:306
  3.3 0.3 slice.33
  3.6 0.0 slice-done
  3.6 0.0 copy-done.9
  3.6 0.1 multiply_bitcast_fusion
  3.6 0.0 copy-done.7
  3.7 0.0 copy-start
  3.7 0.0 copy-start.1
  3.7 0.0 copy-start.2
  3.7 0.0 copy-start.3
  3.7 0.0 copy-start.4
  3.7 0.0 copy-start.5
  3.7 0.0 copy-start.6
  3.7 0.6 fusion
  4.4 0.3 copy-done
  4.6 0.1 copy-done.1
  4.7 0.1 copy-done.2
  4.8 0.0 copy-done.3
  4.8 0.0 copy-done.4
  4.8 30.1 %shard_map.121 = (f32[4,512,128]{2,1,0:T(8,128)S(1)}, f32[32,10,128]{2,1,0:T(8,128)S(1)}) custom-call(f32[512,128]{1,0:T(8,128)S(1)} %get-tuple-element.23.share_ref, f32[512,128]{1,0:T(8,128)S(1)} %bitcast.13, f32[512,128]{1,0:T(8,128)S(1)} %bitcast.15, s32[512,128]{1,0:T(8,128)S(1)} %bitcast.17, s32[1,512]{1,0:T(1,128)S(1)} %bitcast.19, s32[1,512]{1,0:T(1,128)S(1)} %bitcast.21), custom_call_target="tpu_custom_call" | custom-call | tf_op jit(solution)/shard_map/pallas_call | solution.py:340
  34.9 0.0 copy-done.5
  34.9 0.0 copy-done.6
  34.9 19.4 %shard_map.122.river_ref = f32[32,12,128]{2,1,0:T(8,128)S(1)} custom-call(f32[32,10,128]{2,1,0:T(8,128)S(1)} %get-tuple-element.19.agg_ref, f32[1,128]{1,0:T(1,128)S(1)} %copy-done.5, f32[1,128]{1,0:T(1,128)S(1)} %copy-done.6), custom_call_target="tpu_custom_call" | custom-call | tf_op jit(solution)/shard_map/pallas_call | solution.py:354
  54.3 6.7 %shard_map.123 = (f32[512,128]{1,0:T(8,128)}, f32[1,128]{1,0:T(1,128)}) custom-call(f32[32,12,128]{2,1,0:T(8,128)S(1)} %shard_map.122.river_ref, f32[512,128]{1,0:T(8,128)S(1)} %bitcast.14, f32[512,128]{1,0:T(8,128)S(1)} %bitcast.16, s32[512,128]{1,0:T(8,128)S(1)} %bitcast.18, s32[1,512]{1,0:T(1,128)S(1)} %bitcast.20, s32[1,512]{1,0:T(1,128)S(1)} %bitcast.22, ...), custom_call_target="tpu_custom_call" | custom-call | tf_op jit(solution)/shard_map/pallas_call | solution.py:372
  61.1 1.5 %fusion.3 = f32[1,65536]{1,0:T(1,128)S(1)} fusion(f32[1,65536]{1,0:T(1,128)} %bitcast.27, f32[6,65536]{1,0:T(8,128)S(1)} %fusion), kind=kLoop, calls=%fused_computation.7 | loop fusion | flops 393216 | bytes 786432 | tf_op jit(solution)/shard_map/add | solution.py:398
  62.6 1.8 %scatter-add.4 = f32[6,65536]{1,0:T(8,128)S(1)} dynamic-update-slice(f32[6,65536]{1,0:T(8,128)S(1)} %fusion, f32[1,65536]{1,0:T(1,128)S(1)} %fusion.3, s32[]{:T(128)} %constant.34.clone.1, s32[]{:T(128)} %constant.34.clone.1) | dynamic-update-slice | bytes 524292 | tf_op jit(solution)/shard_map/scatter-add | solution.py:398
  64.4 0.0 copy-start.8
  64.4 1.3 %copy-done.8 = f32[6,65536]{1,0:T(8,128)} copy-done((f32[6,65536]{1,0:T(8,128)}, f32[6,65536]{1,0:T(8,128)S(1)}, u32[]{:S(2)}) %copy-start.8) | copy-done | bytes 1572888
Async XLA Ops:
  0.6 2.9 %slice-start = ((f32[6,65536]{1,0:T(8,128)}), f32[1,65536]{1,0:T(1,128)S(1)}, s32[]{:S(2)}) async-start(f32[6,65536]{1,0:T(8,128)} %param.12), calls=%async_computation | async-start | bytes 524288 | tf_op jit(solution)/shard_map/slice | solution.py:303
  0.6 2.9 %copy-start.9 = (f32[65536]{0:T(1024)S(1)}, f32[65536]{0:T(1024)}, u32[]{:S(2)}) copy-start(f32[65536]{0:T(1024)} %param.13) | copy-start | bytes 786436
  0.7 3.0 %copy-start.7 = (f32[6,65536]{1,0:T(8,128)S(1)}, f32[6,65536]{1,0:T(8,128)}, u32[]{:S(2)}) copy-start(f32[6,65536]{1,0:T(8,128)} %param.12) | copy-start | bytes 4718596
  3.7 0.9 %copy-start = (f32[65536]{0:T(1024)S(1)}, f32[65536]{0:T(1024)}, u32[]{:S(2)}) copy-start(f32[65536]{0:T(1024)} %param.15) | copy-start | bytes 786436
  3.7 1.0 %copy-start.1 = (f32[65536]{0:T(1024)S(1)}, f32[65536]{0:T(1024)}, u32[]{:S(2)}) copy-start(f32[65536]{0:T(1024)} %param.16) | copy-start | bytes 786436
  3.7 1.1 %copy-start.2 = (s32[65536]{0:T(1024)S(1)}, s32[65536]{0:T(1024)}, u32[]{:S(2)}) copy-start(s32[65536]{0:T(1024)} %param.17) | copy-start | bytes 786436
  3.7 1.1 %copy-start.3 = (s32[512,1]{0,1:T(1,128)S(1)}, s32[512,1]{0,1:T(1,128)}, u32[]{:S(2)}) copy-start(s32[512,1]{0,1:T(1,128)} %param.18) | copy-start | bytes 6148
  3.7 1.1 %copy-start.4 = (s32[512]{0:T(512)S(1)}, s32[512]{0:T(512)}, u32[]{:S(2)}) copy-start(s32[512]{0:T(512)} %param.19) | copy-start | bytes 6148
  3.7 31.2 %copy-start.5 = (f32[1,128]{1,0:T(1,128)S(1)}, f32[1,128]{1,0:T(1,128)}, u32[]{:S(2)}) copy-start(f32[1,128]{1,0:T(1,128)} %volume_ref.1) | copy-start | bytes 1540
  3.7 31.2 %copy-start.6 = (f32[1,128]{1,0:T(1,128)S(1)}, f32[1,128]{1,0:T(1,128)}, u32[]{:S(2)}) copy-start(f32[1,128]{1,0:T(1,128)} %lag_ref.1) | copy-start | bytes 1540
  64.4 1.3 %copy-start.8 = (f32[6,65536]{1,0:T(8,128)}, f32[6,65536]{1,0:T(8,128)S(1)}, u32[]{:S(2)}) copy-start(f32[6,65536]{1,0:T(8,128)S(1)} %scatter-add.4) | copy-start | bytes 4718596
where the time goes:
time: 65.9 us; the launch traced here: 65.7 us
  Pallas kernels  56.3 us (85%)
  other arithmetic  4.76 us (7%)
  local copies, waits for them, and re-layouts  3.92 us (6%)
  between operations  0.79 us (1%)
    pallas_call x1, Pallas kernels, local(): pl.pallas_call(route_kernel, grid=(blocks // rows,), out_shape=(jax.Shape...  30.1 us
    pallas_call x1, Pallas kernels, local(): pl.pallas_call(functools.partial(exchange_kernel, groups, devices), out_s...  19.4 us
    pallas_call x1, Pallas kernels, local(): pl.pallas_call(functools.partial(settle_kernel, groups), grid=(blocks //...  6.75 us
    mul x1, other arithmetic, land_step(): drained = drain_coef * soil_water * soil_water * soil_water  2.61 us
    scatter-add x1, local copies, waits for them, and re-layouts, local(): soil_mid.at[0].add(recharge_share * flooded * (1.0 - soil_mid[0]))  1.85 us
    unnamed x20, local copies, waits for them, and re-layouts  1.8 us
    add x1, other arithmetic, local(): soil_mid.at[0].add(recharge_share * flooded * (1.0 - soil_mid[0]))  1.48 us

commit v1 on v0

--- a/solution.py
+++ b/solution.py
@@ -25,22 +25,54 @@
     return lax.broadcasted_iota(jnp.int32, shape, len(shape) - 1)
 
 
+def ones_where(mask):
+    return mask.astype(jnp.float32).astype(jnp.bfloat16)
+
+
 def pick(values, index):
     return jnp.take_along_axis(values, index, axis=1)
 
 
-def sort_rows(key, lane):
+def sort_rows(key):
     width = key.shape[1]
+    count = width // 8
+    flipped = key.T
+    parts = [flipped[v * 8 : v * 8 + 8] for v in range(count)]
+    line = lax.broadcasted_iota(jnp.int32, parts[0].shape, 0)
     size = 2
     while size <= width:
         step = size // 2
         while step:
-            other = pick(key, lane ^ step)
-            low = ((lane & step) != 0) == ((lane & size) != 0)
-            key = jnp.where(low, jnp.minimum(key, other), jnp.maximum(key, other))
+            after = list(parts)
+            if step < count:
+                for v in range(count):
+                    if v & step:
+                        continue
+                    small = jnp.minimum(parts[v], parts[v | step])
+                    large = jnp.maximum(parts[v], parts[v | step])
+                    if size < count:
+                        falling = bool(v & size)
+                        after[v], after[v | step] = (large, small) if falling else (small, large)
+                    elif size == width:
+                        after[v], after[v | step] = small, large
+                    else:
+                        falling = (line & (size // count)) != 0
+                        after[v] = jnp.where(falling, large, small)
+                        after[v | step] = jnp.where(falling, small, large)
+            else:
+                hop = step // count
+                upper = (line & hop) != 0
+                low = jnp.logical_xor(upper, (line & (size // count)) == 0)
+                for v in range(count):
+                    here = parts[v]
+                    other = jnp.where(upper, pltpu.roll(here, hop, 0), pltpu.roll(here, 8 - hop, 0))
+                    after[v] = jnp.where(low, jnp.minimum(here, other), jnp.maximum(here, other))
+            parts = after
             step //= 2
         size *= 2
-    return key
+    rows = jnp.concatenate(parts, axis=0).T
+    lane = lanes_of(rows.shape)
+    return pick(rows, (lane % count) * 8 + lane // count)
 
 
 def route_kernel(
@@ -52,7 +84,7 @@
     blocks = owner_ref.shape[1]
     lane = lanes_of((rows, width))
     down = down_ref[...]
-    key = sort_rows((down * width + lane).astype(jnp.float32), lane).astype(jnp.int32)
+    key = sort_rows((down * width + lane).astype(jnp.float32)).astype(jnp.int32)
     order = key % width
     target = key // width
     ends = jnp.zeros_like(lane)
@@ -61,7 +93,16 @@
         ends = jnp.where(pick(target, ends + (hop - 1)) <= lane, ends + hop, ends)
         hop //= 2
     square = (width, width)
-    before = (lax.broadcasted_iota(jnp.int32, square, 0) < lanes_of(square)).astype(jnp.bfloat16)
+    first, second = lax.broadcasted_iota(jnp.int32, square, 0), lanes_of(square)
+    before = ones_where(first < second)
+
+    def product(value, ones):
+        return jnp.dot(
+            jnp.concatenate(split(value), axis=1),
+            jnp.concatenate([ones, ones], axis=0),
+            preferred_element_type=jnp.float32,
+        )
+
     share = share_ref[...]
     rate = rate_ref[...]
     storage = storage_ref[...]
@@ -72,23 +113,17 @@
     sums = jnp.zeros((rows, width), jnp.float32)
     column = 0
     for power in powers:
-        value = jnp.sum(power * storage, axis=1, keepdims=True)
-        sums = jnp.where(lane == column, value, sums)
+        sums = sums + product(power * storage, ones_where(second == column))
         column += 1
     for turn in range(SUB):
         release = rate * storage
-        high, low = split(pick(release, order))
-        running = jnp.dot(high, before, preferred_element_type=jnp.float32) + jnp.dot(
-            low, before, preferred_element_type=jnp.float32
-        )
-        upto = pick(running, ends)
+        upto = pick(product(pick(release, order), before), ends)
         upstream = jnp.where(lane == 0, 0.0, upto - pltpu.roll(upto, 1, 1))
         gained = share + upstream
         up_ref[turn] = gained
         storage = storage + gained - release
         for power in powers[: SUB - 1 - turn]:
-            value = jnp.sum(power * gained, axis=1, keepdims=True)
-            sums = jnp.where(lane == column, value, sums)
+            sums = sums + product(power * gained, ones_where(second == column))
             column += 1
     moment_ref[pl.ds(pl.multiple_of(step * rows, rows), rows), :] = sums
 
@@ -111,13 +146,25 @@
         agg_ref[...] = total.reshape(devices, 16, reaches)[:, :MOMENTS, :]
 
 
+def land_step(soil_water, rainfall, drain_coef):
+    top_layer = soil_water[:1]
+    soaked = rainfall - rainfall * top_layer * top_layer
+    drained = drain_coef * soil_water * soil_water * soil_water
+    inflow = jnp.concatenate([soaked, drained[:-1]], axis=0)
+    return soil_water + inflow - drained
+
+
 def exchange_kernel(
     groups,
     devices,
     agg_ref,
     volume_ref,
     lag_ref,
+    soil_ref,
+    coef_ref,
+    rain_ref,
     out_ref,
+    mid_ref,
     landed,
     mine,
     send_sem,
@@ -177,6 +224,14 @@
 
     start(part)
     landed[0] = agg_ref[me]
+    span = math.gcd(soil_ref.shape[1], 2048)
+
+    def land(turn, carry):
+        at = pl.ds(pl.multiple_of(turn * span, span), span)
+        mid_ref[:, at] = land_step(soil_ref[:, at], rain_ref[:, at], coef_ref[:, at])
+        return carry
+
+    lax.fori_loop(0, soil_ref.shape[1] // span, land, 0)
     finish(part)
     mine[pl.ds(0, MOMENTS), :] = jnp.sum(landed[...], axis=0)
     mine[pl.ds(MOMENTS, 1), :] = volume_ref[...]
@@ -299,15 +354,6 @@
     storage_out_ref[...] = storage
 
 
-def land_step(soil_water, rainfall, drain_coef):
-    top_layer = soil_water[0]
-    surface = rainfall * top_layer * top_layer
-    soaked = rainfall - surface
-    drained = drain_coef * soil_water * soil_water * soil_water
-    inflow = jnp.concatenate([soaked[None], drained[:-1]], axis=0)
-    return (soil_water + inflow - drained, surface + drained[-1])
-
-
 def local(
     soil_water,
     rainfall,
@@ -325,8 +371,9 @@
     blocks = block_owner.shape[0]
     width = rainfall.shape[0] // blocks
     reaches = river_storage.shape[1]
-    rows = math.gcd(blocks, 64)
-    soil_mid, runoff = land_step(soil_water, rainfall, drain_coef)
+    rows = math.gcd(blocks, 128)
+    top, deep = soil_water[0], soil_water[-1]
+    runoff = rainfall * top * top + drain_coef[-1] * deep * deep * deep
     share = (runoff / SUB).reshape(blocks, width)
     storage = cell_storage.reshape(blocks, width)
     rate = release_rate.reshape(blocks, width)
@@ -351,11 +398,14 @@
     )(share, storage, rate, down, owner, reach)
 
     vmem = pl.BlockSpec(memory_space=pltpu.VMEM)
-    river = pl.pallas_call(
+    river, soil_mid = pl.pallas_call(
         functools.partial(exchange_kernel, groups, devices),
-        out_shape=jax.ShapeDtypeStruct((devices, MOMENTS + 2, reaches), jnp.float32),
-        in_specs=[vmem] * 3,
-        out_specs=vmem,
+        out_shape=(
+            jax.ShapeDtypeStruct((devices, MOMENTS + 2, reaches), jnp.float32),
+            jax.ShapeDtypeStruct(soil_water.shape, jnp.float32),
+        ),
+        in_specs=[vmem] * 6,
+        out_specs=(vmem, vmem),
         scratch_shapes=[
             pltpu.VMEM((devices, MOMENTS, reaches), jnp.float32),
             pltpu.VMEM((MOMENTS + 2, reaches), jnp.float32),
@@ -367,7 +417,7 @@
         compiler_params=pltpu.CompilerParams(
             collective_id=0, has_side_effects=True, vmem_limit_bytes=40 * 1024 * 1024
         ),
-    )(agg, river_storage, river_lag)
+    )(agg, river_storage, river_lag, soil_water, drain_coef, rainfall[None])
 
     storage_out, section = pl.pallas_call(
         functools.partial(settle_kernel, groups),
@@ -395,7 +445,9 @@
 
     storage_out = storage_out.reshape(-1)
     flooded = storage_out / (storage_out + 1.0)
-    soil_out = soil_mid.at[0].add(recharge_share * flooded * (1.0 - soil_mid[0]))
+    layer = lax.broadcasted_iota(jnp.int32, soil_mid.shape, 0)
+    wetter = recharge_share * flooded[None] * (1.0 - soil_mid)
+    soil_out = jnp.where(layer == 0, soil_mid + wetter, soil_mid)
     return (soil_out, storage_out, section)
 
 

time: 65.9 us -> 45.5 us (0.69)
  Pallas kernels: 56.3 us -> 33.4 us
  local copies, waits for them, and re-layouts: 3.92 us -> 7.32 us
  other arithmetic: 4.76 us -> 3.69 us
    pallas_call x1, Pallas kernels: 30.1 us -> 9.1 us  [local(): pl.pallas_call(route_kernel, grid=(blocks // rows,), out_shape=(jax.Shape...]
    slice x3 -> x2, local copies, waits for them, and re-layouts: 0.28 us -> 4.75 us  [the longest x1 2.73 us: local(): top, deep = (soil_water[0], soil_water[-1])]
    scatter-add x1 -> x0, local copies, waits for them, and re-layouts: 1.85 us -> none  [local(): soil_mid.at[0].add(recharge_share * flooded * (1.0 - soil_mid[0]))]
    pallas_call x1, Pallas kernels: 6.75 us -> 5.06 us  [local(): pl.pallas_call(functools.partial(settle_kernel, groups), grid=(blocks //...]
    select_n x0 -> x1, other arithmetic: none -> 1.66 us  [local(): soil_out = jnp.where(layer == 0, soil_mid + wetter, soil_mid)]
    mul x1, other arithmetic: 2.61 us -> 0.99 us  [local(): wetter = recharge_share * flooded[None] * (1.0 - soil_mid)]
    add x1 -> x0, other arithmetic: 1.48 us -> none  [local(): soil_mid.at[0].add(recharge_share * flooded * (1.0 - soil_mid[0]))]
    reshape x1, other arithmetic: 0.06 us -> 1.03 us  [local(): share = (runoff / SUB).reshape(blocks, width)]
where the time goes in v1:
time: 45.5 us; the launch traced here: 45.2 us
  Pallas kernels  33.4 us (73%)
  local copies, waits for them, and re-layouts  7.32 us (16%)
  other arithmetic  3.69 us (8%)
  between operations  0.82 us (2%)
    pallas_call x1, Pallas kernels, local(): pl.pallas_call(functools.partial(exchange_kernel, groups, devices), out_s...  19.2 us
    pallas_call x1, Pallas kernels, local(): pl.pallas_call(route_kernel, grid=(blocks // rows,), out_shape=(jax.Shape...  9.1 us
    pallas_call x1, Pallas kernels, local(): pl.pallas_call(functools.partial(settle_kernel, groups), grid=(blocks //...  5.06 us
    slice x1, local copies, waits for them, and re-layouts, local(): top, deep = (soil_water[0], soil_water[-1])  2.73 us
    unnamed x22, local copies, waits for them, and re-layouts  2.57 us
    slice x1, local copies, waits for them, and re-layouts, local(): runoff = rainfall * top * top + drain_coef[-1] * deep * deep * deep  2.02 us
    select_n x1, other arithmetic, local(): soil_out = jnp.where(layer == 0, soil_mid + wetter, soil_mid)  1.66 us
    reshape x1, other arithmetic, local(): share = (runoff / SUB).reshape(blocks, width)  1.03 us

profile of v1, /device:TPU:0, one launch (start us, length us, event | category | flops | bytes accessed | tf_op | source)
XLA Modules:
  0.0 45.2 jit_solution(5201638195921339047)
XLA Ops:
  0.6 0.0 copy-start.2
  0.6 0.0 copy-start
  0.7 0.0 copy-start.10
  0.7 0.0 copy-start.9
  0.7 0.0 copy-start.8
  0.7 0.0 copy-start.7
  0.7 0.0 copy-start.4
  0.7 0.0 copy-start.3
  0.7 2.0 %slice.10 = f32[1,65536]{1,0:T(1,128)S(1)} slice(f32[6,65536]{1,0:T(8,128)} %coef_ref.1), slice={[5:6], [0:65536]} | slice | bytes 524288 | tf_op jit(solution)/shard_map/slice | solution.py:376
  2.7 2.7 %fusion.4 = (f32[1,65536]{1,0:T(1,128)S(1)}, f32[1,65536]{1,0:T(1,128)S(1)}) fusion(f32[6,65536]{1,0:T(8,128)} %soil_ref.1), kind=kLoop, calls=%fused_computation.9 | loop fusion | bytes 1048576 | tf_op jit(solution)/shard_map/slice | solution.py:375
  5.5 1.0 %fusion.2.share_ref = f32[512,128]{1,0:T(8,128)S(1)} fusion(f32[65536]{0:T(1024)S(1)} %bitcast.26, f32[65536]{0:T(1024)} %param.11, f32[65536]{0:T(1024)S(1)} %bitcast.25, f32[65536]{0:T(1024)S(1)} %bitcast.24), kind=kLoop, calls=%fused_computation.6 | loop fusion | flops 458752 | bytes 1310720 | tf_op jit(solution)/shard_map/reshape | solution.py:377
  6.5 0.0 copy-done.8
  6.5 0.0 copy-done.7
  6.5 0.0 copy-done.4
  6.5 0.0 copy-done.3
  6.6 0.0 copy-start.5
  6.6 0.9 %copy-done.5 = s32[65536]{0:T(1024)S(1)} copy-done((s32[65536]{0:T(1024)S(1)}, s32[65536]{0:T(1024)}, u32[]{:S(2)}) %copy-start.5) | copy-done | bytes 262168
  7.5 9.1 %shard_map.121 = (f32[4,512,128]{2,1,0:T(8,128)S(1)}, f32[32,10,128]{2,1,0:T(8,128)S(1)}) custom-call(f32[512,128]{1,0:T(8,128)S(1)} %fusion.2.share_ref, f32[512,128]{1,0:T(8,128)S(1)} %bitcast.14, f32[512,128]{1,0:T(8,128)S(1)} %bitcast.16, s32[512,128]{1,0:T(8,128)S(1)} %bitcast.18, s32[1,512]{1,0:T(1,128)S(1)} %bitcast.20, s32[1,512]{1,0:T(1,128)S(1)} %bitcast.22), custom_call_target="tpu_custom_call" | custom-call | tf_op jit(solution)/shard_map/pallas_call | solution.py:387
  16.6 0.0 copy-done.2
  16.6 0.0 copy-done
  16.6 0.0 copy-done.10
  16.7 0.0 copy-done.9
  16.7 0.0 copy-start.1
  16.7 1.6 %copy-done.1 = f32[6,65536]{1,0:T(8,128)S(1)} copy-done((f32[6,65536]{1,0:T(8,128)S(1)}, f32[6,65536]{1,0:T(8,128)}, u32[]{:S(2)}) %copy-start.1) | copy-done | bytes 1572888
  18.3 0.0 copy-start.6
  18.3 19.2 %shard_map.122 = (f32[32,12,128]{2,1,0:T(8,128)S(1)}, f32[6,65536]{1,0:T(8,128)S(1)}) custom-call(f32[32,10,128]{2,1,0:T(8,128)S(1)} %get-tuple-element.9.agg_ref, f32[1,128]{1,0:T(1,128)S(1)} %copy-done.9, f32[1,128]{1,0:T(1,128)S(1)} %copy-done.10, f32[6,65536]{1,0:T(8,128)S(1)} %copy-done, f32[6,65536]{1,0:T(8,128)S(1)} %copy-done.1, f32[1,65536]{1,0:T(1,128)S(1)} %bitcast.13), custom_call_target="tpu_custom_call" | custom-call | tf_op jit(solution)/shard_map/pallas_call | solution.py:401
  37.5 0.0 copy-done.6
  37.5 5.1 %shard_map.123 = (f32[512,128]{1,0:T(8,128)}, f32[1,128]{1,0:T(1,128)}) custom-call(f32[32,12,128]{2,1,0:T(8,128)S(1)} %get-tuple-element.11.river_ref, f32[512,128]{1,0:T(8,128)S(1)} %bitcast.15, f32[512,128]{1,0:T(8,128)S(1)} %bitcast.17, s32[512,128]{1,0:T(8,128)S(1)} %bitcast.19, s32[1,512]{1,0:T(1,128)S(1)} %bitcast.21, s32[1,512]{1,0:T(1,128)S(1)} %bitcast.23, ...), custom_call_target="tpu_custom_call" | custom-call | tf_op jit(solution)/shard_map/pallas_call | solution.py:422
  42.6 1.0 %fusion.3 = f32[65536]{0:T(1024)S(1)} fusion(f32[512,128]{1,0:T(8,128)} %get-tuple-element.13), kind=kLoop, calls=%fused_computation.7 | loop fusion | flops 196608 | bytes 524288 | tf_op jit(solution)/shard_map/mul | solution.py:449
  43.6 1.7 %add_select_fusion = f32[6,65536]{1,0:T(8,128)} fusion(f32[6,65536]{1,0:T(8,128)S(1)} %get-tuple-element.10, f32[65536]{0:T(1024)S(1)} %fusion.3, pred[6]{0:T(512)(128)(4,1)S(1)} %iota_compare_fusion), kind=kLoop, calls=%fused_computation | loop fusion | flops 1572864 | bytes 3407878 | tf_op jit(solution)/shard_map/jit(_where)/select_n | solution.py:450
  (1 shorter events, 0.0 us)
Async XLA Ops:
  0.6 16.0 %copy-start.2 = (f32[65536]{0:T(1024)S(1)}, f32[65536]{0:T(1024)}, u32[]{:S(2)}) copy-start(f32[65536]{0:T(1024)} %param.11) | copy-start | bytes 786436
  0.6 16.0 %copy-start = (f32[6,65536]{1,0:T(8,128)S(1)}, f32[6,65536]{1,0:T(8,128)}, u32[]{:S(2)}) copy-start(f32[6,65536]{1,0:T(8,128)} %soil_ref.1) | copy-start | bytes 4718596
  0.7 16.0 %copy-start.10 = (f32[1,128]{1,0:T(1,128)S(1)}, f32[1,128]{1,0:T(1,128)}, u32[]{:S(2)}) copy-start(f32[1,128]{1,0:T(1,128)} %lag_ref.1) | copy-start | bytes 1540
  0.7 16.0 %copy-start.9 = (f32[1,128]{1,0:T(1,128)S(1)}, f32[1,128]{1,0:T(1,128)}, u32[]{:S(2)}) copy-start(f32[1,128]{1,0:T(1,128)} %volume_ref.1) | copy-start | bytes 1540
  0.7 5.8 %copy-start.8 = (s32[512]{0:T(512)S(1)}, s32[512]{0:T(512)}, u32[]{:S(2)}) copy-start(s32[512]{0:T(512)} %param.17) | copy-start | bytes 6148
  0.7 5.8 %copy-start.7 = (s32[512,1]{0,1:T(1,128)S(1)}, s32[512,1]{0,1:T(1,128)}, u32[]{:S(2)}) copy-start(s32[512,1]{0,1:T(1,128)} %param.16) | copy-start | bytes 6148
  0.7 5.8 %copy-start.4 = (f32[65536]{0:T(1024)S(1)}, f32[65536]{0:T(1024)}, u32[]{:S(2)}) copy-start(f32[65536]{0:T(1024)} %param.14) | copy-start | bytes 786436
  0.7 5.8 %copy-start.3 = (f32[65536]{0:T(1024)S(1)}, f32[65536]{0:T(1024)}, u32[]{:S(2)}) copy-start(f32[65536]{0:T(1024)} %param.13) | copy-start | bytes 786436
  6.6 1.0 %copy-start.5 = (s32[65536]{0:T(1024)S(1)}, s32[65536]{0:T(1024)}, u32[]{:S(2)}) copy-start(s32[65536]{0:T(1024)} %param.15) | copy-start | bytes 786436
  16.7 1.6 %copy-start.1 = (f32[6,65536]{1,0:T(8,128)S(1)}, f32[6,65536]{1,0:T(8,128)}, u32[]{:S(2)}) copy-start(f32[6,65536]{1,0:T(8,128)} %coef_ref.1) | copy-start | bytes 4718596
  18.3 19.2 %copy-start.6 = (s32[65536]{0:T(1024)S(1)}, s32[65536]{0:T(1024)}, u32[]{:S(2)}) copy-start(s32[65536]{0:T(1024)} %param.15) | copy-start | bytes 786436

commit v2 on v1

--- a/solution.py
+++ b/solution.py
@@ -76,10 +76,23 @@
 
 
 def route_kernel(
-    share_ref, storage_ref, rate_ref, down_ref, owner_ref, reach_ref, up_ref, agg_ref, moment_ref
+    soil_ref,
+    coef_ref,
+    rain_ref,
+    storage_ref,
+    rate_ref,
+    down_ref,
+    owner_ref,
+    reach_ref,
+    up_ref,
+    agg_ref,
+    moment_ref,
+    top_ref,
+    deep_ref,
+    drain_ref,
 ):
     step = pl.program_id(0)
-    rows, width = share_ref.shape
+    rows, width = storage_ref.shape
     devices, _, reaches = agg_ref.shape
     blocks = owner_ref.shape[1]
     lane = lanes_of((rows, width))
@@ -103,7 +116,15 @@
             preferred_element_type=jnp.float32,
         )
 
-    share = share_ref[...]
+    final = soil_ref.shape[0] - 1
+    for b in range(rows):
+        at = slice(b * width, (b + 1) * width)
+        top_ref[b : b + 1, :] = soil_ref[0:1, at]
+        deep_ref[b : b + 1, :] = soil_ref[final : final + 1, at]
+        drain_ref[b : b + 1, :] = coef_ref[final : final + 1, at]
+    top, deep = top_ref[...], deep_ref[...]
+    runoff = rain_ref[...] * top * top + drain_ref[...] * deep * deep * deep
+    share = runoff / SUB
     rate = rate_ref[...]
     storage = storage_ref[...]
     leaving = jnp.where(down == width, rate, 0.0)
@@ -160,11 +181,15 @@
     agg_ref,
     volume_ref,
     lag_ref,
+    soil_hbm,
+    coef_hbm,
+    rain_hbm,
+    out_ref,
+    mid_ref,
     soil_ref,
     coef_ref,
     rain_ref,
-    out_ref,
-    mid_ref,
+    load_sem,
     landed,
     mine,
     send_sem,
@@ -178,6 +203,13 @@
         peer = lax.rem(me + step, devices)
         return peer, (peer // groups, lax.rem(peer, groups))
 
+    loads = [
+        pltpu.make_async_copy(soil_hbm, soil_ref, load_sem.at[0]),
+        pltpu.make_async_copy(coef_hbm, coef_ref, load_sem.at[1]),
+        pltpu.make_async_copy(rain_hbm, rain_ref, load_sem.at[2]),
+    ]
+    for load in loads:
+        load.start()
     barrier = pltpu.get_barrier_semaphore()
 
     def greet(step, carry):
@@ -231,6 +263,8 @@
         mid_ref[:, at] = land_step(soil_ref[:, at], rain_ref[:, at], coef_ref[:, at])
         return carry
 
+    for load in loads:
+        load.wait()
     lax.fori_loop(0, soil_ref.shape[1] // span, land, 0)
     finish(part)
     mine[pl.ds(0, MOMENTS), :] = jnp.sum(landed[...], axis=0)
@@ -302,10 +336,13 @@
     owner_ref,
     reach_ref,
     up_ref,
+    mid_ref,
     storage_out_ref,
     section_ref,
+    soil_out_ref,
     table_ref,
     place_ref,
+    wet_ref,
 ):
     step = pl.program_id(0)
     rows, width = storage_ref.shape
@@ -352,6 +389,12 @@
         release = rate * storage * jnp.where(leaving, back, 1.0)
         storage = storage + up_ref[turn] - release
     storage_out_ref[...] = storage
+    wet_ref[...] = recharge_share * (storage / (storage + 1.0))
+    soil_out_ref[1:, :] = mid_ref[1:, :]
+    for b in range(rows):
+        at = slice(b * width, (b + 1) * width)
+        top = mid_ref[0:1, at]
+        soil_out_ref[0:1, at] = top + wet_ref[b : b + 1, :] * (1.0 - top)
 
 
 def local(
@@ -372,9 +415,7 @@
     width = rainfall.shape[0] // blocks
     reaches = river_storage.shape[1]
     rows = math.gcd(blocks, 128)
-    top, deep = soil_water[0], soil_water[-1]
-    runoff = rainfall * top * top + drain_coef[-1] * deep * deep * deep
-    share = (runoff / SUB).reshape(blocks, width)
+    rain = rainfall.reshape(blocks, width)
     storage = cell_storage.reshape(blocks, width)
     rate = release_rate.reshape(blocks, width)
     down = downstream.reshape(blocks, width)
@@ -382,6 +423,8 @@
     reach = outlet_reach.reshape(1, blocks)
 
     tile = pl.BlockSpec((rows, width), lambda i: (i, 0))
+    layers = soil_water.shape[0]
+    slab = pl.BlockSpec((layers, rows * width), lambda i: (0, i))
     line = pl.BlockSpec((1, blocks), lambda i: (0, 0))
     stack = pl.BlockSpec((SUB, rows, width), lambda i: (0, i, 0))
     gained, agg = pl.pallas_call(
@@ -391,11 +434,12 @@
             jax.ShapeDtypeStruct((SUB, blocks, width), jnp.float32),
             jax.ShapeDtypeStruct((devices, MOMENTS, reaches), jnp.float32),
         ),
-        in_specs=[tile, tile, tile, tile, line, line],
+        in_specs=[slab, slab, tile, tile, tile, tile, line, line],
         out_specs=(stack, pl.BlockSpec((devices, MOMENTS, reaches), lambda i: (0, 0, 0))),
-        scratch_shapes=[pltpu.VMEM((blocks, width), jnp.float32)],
+        scratch_shapes=[pltpu.VMEM((blocks, width), jnp.float32)]
+        + [pltpu.VMEM((rows, width), jnp.float32)] * 3,
         compiler_params=pltpu.CompilerParams(vmem_limit_bytes=40 * 1024 * 1024),
-    )(share, storage, rate, down, owner, reach)
+    )(soil_water, drain_coef, rain, storage, rate, down, owner, reach)
 
     vmem = pl.BlockSpec(memory_space=pltpu.VMEM)
     river, soil_mid = pl.pallas_call(
@@ -404,9 +448,13 @@
             jax.ShapeDtypeStruct((devices, MOMENTS + 2, reaches), jnp.float32),
             jax.ShapeDtypeStruct(soil_water.shape, jnp.float32),
         ),
-        in_specs=[vmem] * 6,
+        in_specs=[vmem] * 3 + [pl.BlockSpec(memory_space=pl.ANY)] * 3,
         out_specs=(vmem, vmem),
         scratch_shapes=[
+            pltpu.VMEM(soil_water.shape, jnp.float32),
+            pltpu.VMEM(soil_water.shape, jnp.float32),
+            pltpu.VMEM((1, soil_water.shape[1]), jnp.float32),
+            pltpu.SemaphoreType.DMA((3,)),
             pltpu.VMEM((devices, MOMENTS, reaches), jnp.float32),
             pltpu.VMEM((MOMENTS + 2, reaches), jnp.float32),
             pltpu.SemaphoreType.DMA((devices,)),
@@ -419,12 +467,13 @@
         ),
     )(agg, river_storage, river_lag, soil_water, drain_coef, rainfall[None])
 
-    storage_out, section = pl.pallas_call(
+    storage_out, section, soil_out = pl.pallas_call(
         functools.partial(settle_kernel, groups),
         grid=(blocks // rows,),
         out_shape=(
             jax.ShapeDtypeStruct((blocks, width), jnp.float32),
             jax.ShapeDtypeStruct((1, reaches), jnp.float32),
+            jax.ShapeDtypeStruct(soil_water.shape, jnp.float32),
         ),
         in_specs=[
             pl.BlockSpec((devices, MOMENTS + 2, reaches), lambda i: (0, 0, 0)),
@@ -434,21 +483,18 @@
             line,
             line,
             stack,
+            slab,
         ],
-        out_specs=(tile, pl.BlockSpec((1, reaches), lambda i: (0, 0))),
+        out_specs=(tile, pl.BlockSpec((1, reaches), lambda i: (0, 0)), slab),
         scratch_shapes=[
             pltpu.VMEM((2, devices, SUB * reaches), jnp.bfloat16),
             pltpu.VMEM((blocks, 128), jnp.float32),
+            pltpu.VMEM((rows, width), jnp.float32),
         ],
         compiler_params=pltpu.CompilerParams(vmem_limit_bytes=40 * 1024 * 1024),
-    )(river, storage, rate, down, owner, reach, gained)
-
-    storage_out = storage_out.reshape(-1)
-    flooded = storage_out / (storage_out + 1.0)
-    layer = lax.broadcasted_iota(jnp.int32, soil_mid.shape, 0)
-    wetter = recharge_share * flooded[None] * (1.0 - soil_mid)
-    soil_out = jnp.where(layer == 0, soil_mid + wetter, soil_mid)
-    return (soil_out, storage_out, section)
+    )(river, storage, rate, down, owner, reach, gained, soil_mid)
+
+    return (soil_out, storage_out.reshape(-1), section)
 
 
 def solution(mesh):

time: 45.5 us -> 44.2 us (0.971)
  other arithmetic: 3.69 us -> 0 us
  Pallas kernels: 33.4 us -> 34.7 us
  local copies, waits for them, and re-layouts: 7.32 us -> 8.37 us
    unnamed x22 -> x30, local copies, waits for them, and re-layouts: 2.57 us -> 8.37 us
    slice x2 -> x0, local copies, waits for them, and re-layouts: 4.75 us -> none  [the longest x1 2.73 us: local(): top, deep = (soil_water[0], soil_water[-1])]
    select_n x1 -> x0, other arithmetic: 1.66 us -> none  [local(): soil_out = jnp.where(layer == 0, soil_mid + wetter, soil_mid)]
    reshape x1 -> x0, other arithmetic: 1.03 us -> none  [local(): share = (runoff / SUB).reshape(blocks, width)]
    mul x1 -> x0, other arithmetic: 0.99 us -> none  [local(): wetter = recharge_share * flooded[None] * (1.0 - soil_mid)]
    pallas_call x1, Pallas kernels: 5.06 us -> 5.81 us  [local(): pl.pallas_call(functools.partial(settle_kernel, groups), grid=(blocks //...]
    pallas_call x1, Pallas kernels: 19.2 us -> 19.8 us  [local(): pl.pallas_call(functools.partial(exchange_kernel, groups, devices), out_s...]
where the time goes in v2:
time: 44.2 us; the launch traced here: 43.8 us
  Pallas kernels  34.7 us (79%)
  local copies, waits for them, and re-layouts  8.37 us (19%)
  between operations  0.76 us (2%)
    pallas_call x1, Pallas kernels, local(): pl.pallas_call(functools.partial(exchange_kernel, groups, devices), out_s...  19.8 us
    pallas_call x1, Pallas kernels, local(): pl.pallas_call(route_kernel, grid=(blocks // rows,), out_shape=(jax.Shape...  9.14 us
    unnamed x30, local copies, waits for them, and re-layouts  8.37 us
    pallas_call x1, Pallas kernels, local(): pl.pallas_call(functools.partial(settle_kernel, groups), grid=(blocks //...  5.81 us

profile of v2, /device:TPU:0, one launch (start us, length us, event | category | flops | bytes accessed | tf_op | source)
XLA Modules:
  0.0 43.8 jit_solution(9313741359818676985)
XLA Ops:
  0.6 0.0 copy-start
  0.6 1.6 %copy-done = f32[6,65536]{1,0:T(8,128)S(1)} copy-done((f32[6,65536]{1,0:T(8,128)S(1)}, f32[6,65536]{1,0:T(8,128)}, u32[]{:S(2)}) %copy-start) | copy-done | bytes 1572888
  2.2 0.0 copy-start.1
  2.2 1.6 %copy-done.1 = f32[6,65536]{1,0:T(8,128)S(1)} copy-done((f32[6,65536]{1,0:T(8,128)S(1)}, f32[6,65536]{1,0:T(8,128)}, u32[]{:S(2)}) %copy-start.1) | copy-done | bytes 1572888
  3.8 0.0 copy-start.2
  3.8 0.9 %copy-done.2 = f32[65536]{0:T(1024)S(1)} copy-done((f32[65536]{0:T(1024)S(1)}, f32[65536]{0:T(1024)}, u32[]{:S(2)}) %copy-start.2) | copy-done | bytes 262168
  4.8 0.0 copy-start.3
  4.8 0.9 %copy-done.3 = f32[65536]{0:T(1024)S(1)} copy-done((f32[65536]{0:T(1024)S(1)}, f32[65536]{0:T(1024)}, u32[]{:S(2)}) %copy-start.3) | copy-done | bytes 262168
  5.7 0.0 copy-start.5
  5.7 0.9 %copy-done.5 = f32[65536]{0:T(1024)S(1)} copy-done((f32[65536]{0:T(1024)S(1)}, f32[65536]{0:T(1024)}, u32[]{:S(2)}) %copy-start.5) | copy-done | bytes 262168
  6.7 0.0 copy-start.7
  6.7 0.9 %copy-done.7 = s32[65536]{0:T(1024)S(1)} copy-done((s32[65536]{0:T(1024)S(1)}, s32[65536]{0:T(1024)}, u32[]{:S(2)}) %copy-start.7) | copy-done | bytes 262168
  7.6 0.0 copy-start.9
  7.6 0.7 %copy-done.9 = s32[512,1]{0,1:T(1,128)S(1)} copy-done((s32[512,1]{0,1:T(1,128)S(1)}, s32[512,1]{0,1:T(1,128)}, u32[]{:S(2)}) %copy-start.9) | copy-done | bytes 2072
  8.3 0.0 copy-start.11
  8.3 0.7 %copy-done.11 = s32[512]{0:T(512)S(1)} copy-done((s32[512]{0:T(512)S(1)}, s32[512]{0:T(512)}, u32[]{:S(2)}) %copy-start.11) | copy-done | bytes 2072
  9.0 0.0 copy-start.13
  9.0 0.0 copy-start.14
  9.0 9.1 %shard_map.121 = (f32[4,512,128]{2,1,0:T(8,128)S(1)}, f32[32,10,128]{2,1,0:T(8,128)S(1)}) custom-call(f32[6,65536]{1,0:T(8,128)S(1)} %copy-done, f32[6,65536]{1,0:T(8,128)S(1)} %copy-done.1, f32[512,128]{1,0:T(8,128)S(1)} %bitcast.8, f32[512,128]{1,0:T(8,128)S(1)} %bitcast.10, f32[512,128]{1,0:T(8,128)S(1)} %bitcast.12, s32[512,128]{1,0:T(8,128)S(1)} %bitcast.14, ...), custom_call_target="tpu_custom_call" | custom-call | tf_op jit(solution)/shard_map/pallas_call | solution.py:430
  18.1 0.0 copy-done.13
  18.1 0.0 copy-done.14
  18.2 0.0 copy-start.4
  18.2 0.0 copy-start.6
  18.2 0.0 copy-start.8
  18.2 0.0 copy-start.10
  18.2 0.0 copy-start.12
  18.2 19.8 %shard_map.122 = (f32[32,12,128]{2,1,0:T(8,128)S(1)}, f32[6,65536]{1,0:T(8,128)S(1)}) custom-call(f32[32,10,128]{2,1,0:T(8,128)S(1)} %get-tuple-element.10.agg_ref, f32[1,128]{1,0:T(1,128)S(1)} %copy-done.13, f32[1,128]{1,0:T(1,128)S(1)} %copy-done.14, f32[6,65536]{1,0:T(8,128)S(1)} %copy-done, f32[6,65536]{1,0:T(8,128)S(1)} %copy-done.1, f32[1,65536]{1,0:T(1,128)S(1)} %bitcast.9), custom_call_target="tpu_custom_call" | custom-call | tf_op jit(solution)/shard_map/pallas_call | solution.py:445
  38.0 0.0 copy-done.4
  38.0 0.0 copy-done.6
  38.0 0.0 copy-done.8
  38.0 0.0 copy-done.10
  38.0 0.0 copy-done.12
  38.0 5.8 %shard_map.123 = (f32[512,128]{1,0:T(8,128)}, f32[1,128]{1,0:T(1,128)}, f32[6,65536]{1,0:T(8,128)}) custom-call(f32[32,12,128]{2,1,0:T(8,128)S(1)} %get-tuple-element.11.river_ref, f32[512,128]{1,0:T(8,128)S(1)} %bitcast.11, f32[512,128]{1,0:T(8,128)S(1)} %bitcast.13, s32[512,128]{1,0:T(8,128)S(1)} %bitcast.15, s32[1,512]{1,0:T(1,128)S(1)} %bitcast.17, ...), custom_call_target="tpu_custom_call" | custom-call | tf_op jit(solution)/shard_map/pallas_call | solution.py:470
Async XLA Ops:
  0.6 1.6 %copy-start = (f32[6,65536]{1,0:T(8,128)S(1)}, f32[6,65536]{1,0:T(8,128)}, u32[]{:S(2)}) copy-start(f32[6,65536]{1,0:T(8,128)} %soil_hbm.1) | copy-start | bytes 4718596
  2.2 1.6 %copy-start.1 = (f32[6,65536]{1,0:T(8,128)S(1)}, f32[6,65536]{1,0:T(8,128)}, u32[]{:S(2)}) copy-start(f32[6,65536]{1,0:T(8,128)} %coef_hbm.1) | copy-start | bytes 4718596
  3.8 0.9 %copy-start.2 = (f32[65536]{0:T(1024)S(1)}, f32[65536]{0:T(1024)}, u32[]{:S(2)}) copy-start(f32[65536]{0:T(1024)} %param.11) | copy-start | bytes 786436
  4.8 0.9 %copy-start.3 = (f32[65536]{0:T(1024)S(1)}, f32[65536]{0:T(1024)}, u32[]{:S(2)}) copy-start(f32[65536]{0:T(1024)} %param.13) | copy-start | bytes 786436
  5.7 0.9 %copy-start.5 = (f32[65536]{0:T(1024)S(1)}, f32[65536]{0:T(1024)}, u32[]{:S(2)}) copy-start(f32[65536]{0:T(1024)} %param.14) | copy-start | bytes 786436
  6.7 0.9 %copy-start.7 = (s32[65536]{0:T(1024)S(1)}, s32[65536]{0:T(1024)}, u32[]{:S(2)}) copy-start(s32[65536]{0:T(1024)} %param.15) | copy-start | bytes 786436
  7.6 0.7 %copy-start.9 = (s32[512,1]{0,1:T(1,128)S(1)}, s32[512,1]{0,1:T(1,128)}, u32[]{:S(2)}) copy-start(s32[512,1]{0,1:T(1,128)} %param.16) | copy-start | bytes 6148
  8.3 0.7 %copy-start.11 = (s32[512]{0:T(512)S(1)}, s32[512]{0:T(512)}, u32[]{:S(2)}) copy-start(s32[512]{0:T(512)} %param.17) | copy-start | bytes 6148
  9.0 9.2 %copy-start.13 = (f32[1,128]{1,0:T(1,128)S(1)}, f32[1,128]{1,0:T(1,128)}, u32[]{:S(2)}) copy-start(f32[1,128]{1,0:T(1,128)} %volume_ref.1) | copy-start | bytes 1540
  9.0 9.2 %copy-start.14 = (f32[1,128]{1,0:T(1,128)S(1)}, f32[1,128]{1,0:T(1,128)}, u32[]{:S(2)}) copy-start(f32[1,128]{1,0:T(1,128)} %lag_ref.1) | copy-start | bytes 1540
  18.2 19.8 %copy-start.4 = (f32[65536]{0:T(1024)S(1)}, f32[65536]{0:T(1024)}, u32[]{:S(2)}) copy-start(f32[65536]{0:T(1024)} %param.13) | copy-start | bytes 786436
  18.2 19.8 %copy-start.6 = (f32[65536]{0:T(1024)S(1)}, f32[65536]{0:T(1024)}, u32[]{:S(2)}) copy-start(f32[65536]{0:T(1024)} %param.14) | copy-start | bytes 786436
  18.2 19.8 %copy-start.8 = (s32[65536]{0:T(1024)S(1)}, s32[65536]{0:T(1024)}, u32[]{:S(2)}) copy-start(s32[65536]{0:T(1024)} %param.15) | copy-start | bytes 786436
  18.2 19.8 %copy-start.10 = (s32[512,1]{0,1:T(1,128)S(1)}, s32[512,1]{0,1:T(1,128)}, u32[]{:S(2)}) copy-start(s32[512,1]{0,1:T(1,128)} %param.16) | copy-start | bytes 6148
  18.2 19.8 %copy-start.12 = (s32[512]{0:T(512)S(1)}, s32[512]{0:T(512)}, u32[]{:S(2)}) copy-start(s32[512]{0:T(512)} %param.17) | copy-start | bytes 6148

commit v3 on v2

--- a/solution.py
+++ b/solution.py
@@ -438,7 +438,7 @@
         out_specs=(stack, pl.BlockSpec((devices, MOMENTS, reaches), lambda i: (0, 0, 0))),
         scratch_shapes=[pltpu.VMEM((blocks, width), jnp.float32)]
         + [pltpu.VMEM((rows, width), jnp.float32)] * 3,
-        compiler_params=pltpu.CompilerParams(vmem_limit_bytes=40 * 1024 * 1024),
+        compiler_params=pltpu.CompilerParams(vmem_limit_bytes=63 * 1024 * 1024),
     )(soil_water, drain_coef, rain, storage, rate, down, owner, reach)
 
     vmem = pl.BlockSpec(memory_space=pltpu.VMEM)
@@ -463,7 +463,7 @@
             pltpu.SemaphoreType.DMA((devices,)),
         ],
         compiler_params=pltpu.CompilerParams(
-            collective_id=0, has_side_effects=True, vmem_limit_bytes=40 * 1024 * 1024
+            collective_id=0, has_side_effects=True, vmem_limit_bytes=63 * 1024 * 1024
         ),
     )(agg, river_storage, river_lag, soil_water, drain_coef, rainfall[None])
 
@@ -491,7 +491,7 @@
             pltpu.VMEM((blocks, 128), jnp.float32),
             pltpu.VMEM((rows, width), jnp.float32),
         ],
-        compiler_params=pltpu.CompilerParams(vmem_limit_bytes=40 * 1024 * 1024),
+        compiler_params=pltpu.CompilerParams(vmem_limit_bytes=63 * 1024 * 1024),
     )(river, storage, rate, down, owner, reach, gained, soil_mid)
 
     return (soil_out, storage_out.reshape(-1), section)

time: 44.2 us -> 41.6 us (0.941)
  local copies, waits for them, and re-layouts: 8.37 us -> 0 us
  Pallas kernels: 34.7 us -> 40.7 us
    unnamed x30 -> x0, local copies, waits for them, and re-layouts: 8.37 us -> none
    pallas_call x1, Pallas kernels: 9.14 us -> 11.3 us  [local(): pl.pallas_call(route_kernel, grid=(blocks // rows,), out_shape=(jax.Shape...]
    pallas_call x1, Pallas kernels: 19.8 us -> 21.7 us  [local(): pl.pallas_call(functools.partial(exchange_kernel, groups, devices), out_s...]
    pallas_call x1, Pallas kernels: 5.81 us -> 7.7 us  [local(): pl.pallas_call(functools.partial(settle_kernel, groups), grid=(blocks //...]
where the time goes in v3:
time: 41.6 us; the launch traced here: 41.3 us
  Pallas kernels  40.7 us (98%)
  between operations  0.64 us (2%)
    pallas_call x1, Pallas kernels, local(): pl.pallas_call(functools.partial(exchange_kernel, groups, devices), out_s...  21.7 us
    pallas_call x1, Pallas kernels, local(): pl.pallas_call(route_kernel, grid=(blocks // rows,), out_shape=(jax.Shape...  11.3 us
    pallas_call x1, Pallas kernels, local(): pl.pallas_call(functools.partial(settle_kernel, groups), grid=(blocks //...  7.7 us

profile of v3, /device:TPU:0, one launch (start us, length us, event | category | flops | bytes accessed | tf_op | source)
XLA Modules:
  0.0 41.3 jit_solution(1626081770814123031)
XLA Ops:
  0.6 11.3 %shard_map.121 = (f32[4,512,128]{2,1,0:T(8,128)}, f32[32,10,128]{2,1,0:T(8,128)}) custom-call(f32[6,65536]{1,0:T(8,128)} %soil_hbm.1, f32[6,65536]{1,0:T(8,128)} %coef_hbm.1, f32[512,128]{1,0:T(8,128)} %bitcast.8, f32[512,128]{1,0:T(8,128)} %bitcast.10, f32[512,128]{1,0:T(8,128)} %bitcast.12, s32[512,128]{1,0:T(8,128)} %bitcast.14, s32[1,512]{1,0:T(1,128)} %bitcast.16, ...), custom_call_target="tpu_custom_call" | custom-call | tf_op jit(solution)/shard_map/pallas_call | solution.py:430
  11.9 21.7 %shard_map.122 = (f32[32,12,128]{2,1,0:T(8,128)}, f32[6,65536]{1,0:T(8,128)}) custom-call(f32[32,10,128]{2,1,0:T(8,128)} %get-tuple-element.10.agg_ref, f32[1,128]{1,0:T(1,128)} %volume_ref.1, f32[1,128]{1,0:T(1,128)} %lag_ref.1, f32[6,65536]{1,0:T(8,128)} %soil_hbm.1, f32[6,65536]{1,0:T(8,128)} %coef_hbm.1, f32[1,65536]{1,0:T(1,128)} %bitcast.9), custom_call_target="tpu_custom_call" | custom-call | tf_op jit(solution)/shard_map/pallas_call | solution.py:445
  33.6 7.7 %shard_map.123 = (f32[512,128]{1,0:T(8,128)}, f32[1,128]{1,0:T(1,128)}, f32[6,65536]{1,0:T(8,128)}) custom-call(f32[32,12,128]{2,1,0:T(8,128)} %get-tuple-element.11.river_ref, f32[512,128]{1,0:T(8,128)} %bitcast.11, f32[512,128]{1,0:T(8,128)} %bitcast.13, s32[512,128]{1,0:T(8,128)} %bitcast.15, s32[1,512]{1,0:T(1,128)} %bitcast.17, s32[1,512]{1,0:T(1,128)} %bitcast.19, ...), custom_call_target="tpu_custom_call" | custom-call | tf_op jit(solution)/shard_map/pallas_call | solution.py:470

commit v4 on v3

--- a/solution.py
+++ b/solution.py
@@ -185,6 +185,7 @@
     coef_hbm,
     rain_hbm,
     out_ref,
+    mid_hbm,
     mid_ref,
     soil_ref,
     coef_ref,
@@ -266,6 +267,8 @@
     for load in loads:
         load.wait()
     lax.fori_loop(0, soil_ref.shape[1] // span, land, 0)
+    store = pltpu.make_async_copy(mid_ref, mid_hbm, load_sem.at[3])
+    store.start()
     finish(part)
     mine[pl.ds(0, MOMENTS), :] = jnp.sum(landed[...], axis=0)
     mine[pl.ds(MOMENTS, 1), :] = volume_ref[...]
@@ -273,6 +276,7 @@
     start(whole)
     out_ref[me] = mine[...]
     finish(whole)
+    store.wait()
 
 
 def simulate(groups, river, width):
@@ -449,12 +453,13 @@
             jax.ShapeDtypeStruct(soil_water.shape, jnp.float32),
         ),
         in_specs=[vmem] * 3 + [pl.BlockSpec(memory_space=pl.ANY)] * 3,
-        out_specs=(vmem, vmem),
+        out_specs=(vmem, pl.BlockSpec(memory_space=pl.ANY)),
         scratch_shapes=[
             pltpu.VMEM(soil_water.shape, jnp.float32),
             pltpu.VMEM(soil_water.shape, jnp.float32),
+            pltpu.VMEM(soil_water.shape, jnp.float32),
             pltpu.VMEM((1, soil_water.shape[1]), jnp.float32),
-            pltpu.SemaphoreType.DMA((3,)),
+            pltpu.SemaphoreType.DMA((4,)),
             pltpu.VMEM((devices, MOMENTS, reaches), jnp.float32),
             pltpu.VMEM((MOMENTS + 2, reaches), jnp.float32),
             pltpu.SemaphoreType.DMA((devices,)),

time: 41.6 us -> 40.8 us (0.981)
  Pallas kernels: 40.7 us -> 40 us
    pallas_call x1, Pallas kernels: 21.7 us -> 20.9 us  [local(): pl.pallas_call(functools.partial(exchange_kernel, groups, devices), out_s...]
where the time goes in v4:
time: 40.8 us; the launch traced here: 40.6 us
  Pallas kernels  40 us (98%)
  between operations  0.64 us (2%)
    pallas_call x1, Pallas kernels, local(): pl.pallas_call(functools.partial(exchange_kernel, groups, devices), out_s...  20.9 us
    pallas_call x1, Pallas kernels, local(): pl.pallas_call(route_kernel, grid=(blocks // rows,), out_shape=(jax.Shape...  11.3 us
    pallas_call x1, Pallas kernels, local(): pl.pallas_call(functools.partial(settle_kernel, groups), grid=(blocks //...  7.7 us

profile of v4, /device:TPU:0, one launch (start us, length us, event | category | flops | bytes accessed | tf_op | source)
XLA Modules:
  0.0 40.6 jit_solution(14690354357373212083)
XLA Ops:
  0.6 11.3 %shard_map.121 = (f32[4,512,128]{2,1,0:T(8,128)}, f32[32,10,128]{2,1,0:T(8,128)}) custom-call(f32[6,65536]{1,0:T(8,128)} %soil_hbm.1, f32[6,65536]{1,0:T(8,128)} %coef_hbm.1, f32[512,128]{1,0:T(8,128)} %bitcast.8, f32[512,128]{1,0:T(8,128)} %bitcast.10, f32[512,128]{1,0:T(8,128)} %bitcast.12, s32[512,128]{1,0:T(8,128)} %bitcast.14, s32[1,512]{1,0:T(1,128)} %bitcast.16, ...), custom_call_target="tpu_custom_call" | custom-call | tf_op jit(solution)/shard_map/pallas_call | solution.py:434
  11.9 20.9 %shard_map.122 = (f32[32,12,128]{2,1,0:T(8,128)}, f32[6,65536]{1,0:T(8,128)}) custom-call(f32[32,10,128]{2,1,0:T(8,128)} %get-tuple-element.10.agg_ref, f32[1,128]{1,0:T(1,128)} %volume_ref.1, f32[1,128]{1,0:T(1,128)} %lag_ref.1, f32[6,65536]{1,0:T(8,128)} %soil_hbm.1, f32[6,65536]{1,0:T(8,128)} %coef_hbm.1, f32[1,65536]{1,0:T(1,128)} %bitcast.9), custom_call_target="tpu_custom_call" | custom-call | tf_op jit(solution)/shard_map/pallas_call | solution.py:449
  32.9 7.7 %shard_map.123 = (f32[512,128]{1,0:T(8,128)}, f32[1,128]{1,0:T(1,128)}, f32[6,65536]{1,0:T(8,128)}) custom-call(f32[32,12,128]{2,1,0:T(8,128)} %get-tuple-element.11.river_ref, f32[512,128]{1,0:T(8,128)} %bitcast.11, f32[512,128]{1,0:T(8,128)} %bitcast.13, s32[512,128]{1,0:T(8,128)} %bitcast.15, s32[1,512]{1,0:T(1,128)} %bitcast.17, s32[1,512]{1,0:T(1,128)} %bitcast.19, ...), custom_call_target="tpu_custom_call" | custom-call | tf_op jit(solution)/shard_map/pallas_call | solution.py:475
